TPU v7x, 256 devices: a whole 4x4x8 slice. The times are simulated.
256 devices in a mesh: blk: 8 (over z_hi, core), head: 32 (over y, z_lo, x).
Axes of the slice: x: 4, y: 4, z: 8 (z_hi: 4, z_lo: 2; z = z_hi * 2 + z_lo), core: 2. Of those that a mesh axis runs over, the one named last changes fastest.
Arguments:
- tokens_qkv: bfloat16 [8192, 12288], P(('blk', 'head')), may hold values from -8 to 8, as said below
- block_mask: int32 [64, 64], replicated, may hold values from 0 to 1, as said below
Outputs:
- attended: bfloat16 [8192, 4096], P(('blk', 'head'))
Inputs may be any that keep to these rules, and one draw needn't show every extreme that they name: `tokens_qkv`: queries, keys and values ordered by head, then query, key, value, then the 128 entries. `block_mask`: 1 where a pair of 128-token blocks attends; a block always attends to itself whatever the entry says.
All inputs are finite; a program needn't handle non-finite values.
Results may differ from a plain program's by a relative error of at most 0.007.
Values may be sent and summed in bfloat16 or wider, within the bound.
A program may use at most 64 MiB of HBM per device.

v0:
```python
import jax
import jax.numpy as jnp
from jax import lax
from jax.sharding import PartitionSpec as P

HD = 128
BLOCK = 128


NEGATIVE = -1e30


def shortened(x):

    def short(part):
        return part.astype(jnp.bfloat16) if part.dtype == jnp.float32 else part

    return jax.tree.map(short, x)


def shifted(x, axis, by):
    size = lax.axis_size(axis)
    return lax.ppermute(x, axis, [(i, (i + by) % size) for i in range(size)])


def live_pairs(block_mask, row_start, row_count, col_start, col_count):
    picked = lax.dynamic_slice(
        block_mask,
        (row_start // BLOCK, col_start // BLOCK),
        (row_count // BLOCK, col_count // BLOCK),
    )
    spread = jnp.broadcast_to(
        (picked == 1)[:, None, :, None], (row_count // BLOCK, BLOCK, col_count // BLOCK, BLOCK)
    ).reshape(row_count, col_count)
    row_blocks = (row_start + jnp.arange(row_count, dtype=jnp.int32)) // BLOCK
    col_blocks = (col_start + jnp.arange(col_count, dtype=jnp.int32)) // BLOCK
    return spread | (row_blocks[:, None] == col_blocks[None, :])


def attend(running, queries, keys_part, values_part, live_map):
    outputs, maxima, totals = running
    key_count = keys_part.shape[0]
    stride = min(key_count, 512)
    factor_scale = queries.shape[-1] ** (-0.5)
    for offset in range(0, key_count, stride):
        scores = (
            jnp.einsum(
                "qhd,khd->qhk",
                queries,
                keys_part[offset : offset + stride],
                preferred_element_type=jnp.float32,
            )
            * factor_scale
        )
        allowed = live_map[:, None, offset : offset + stride]
        scores = jnp.where(allowed, scores, NEGATIVE)
        newest = jnp.maximum(maxima, jnp.max(scores, axis=-1))
        weights = jnp.where(allowed, jnp.exp(scores - newest[..., None]), 0.0)
        factor = jnp.exp(maxima - newest)
        totals = totals * factor + jnp.sum(weights, axis=-1)
        outputs = outputs * factor[..., None] + jnp.einsum(
            "qhk,khd->qhd",
            weights.astype(jnp.bfloat16),
            values_part[offset : offset + stride],
            preferred_element_type=jnp.float32,
        )
        maxima = newest
    return (outputs, maxima, totals)


def empty_state(row_total, head_count):
    return (
        jnp.zeros((row_total, head_count, HD), jnp.float32),
        jnp.full((row_total, head_count), NEGATIVE, jnp.float32),
        jnp.zeros((row_total, head_count), jnp.float32),
    )


def on_device(tokens_qkv, block_mask):
    by_heads = lax.all_to_all(tokens_qkv, "head", split_axis=1, concat_axis=0, tiled=True)
    rows_here = by_heads.shape[0]
    head_count = by_heads.shape[1] // (3 * HD)
    packed = by_heads.reshape(rows_here, head_count, 3, HD)
    queries = packed[:, :, 0]
    keys_here = packed[:, :, 1]
    values_here = packed[:, :, 2]
    cycle_size = lax.axis_size("blk")
    own_index = lax.axis_index("blk")
    own_start = own_index * rows_here
    running = attend(
        empty_state(rows_here, head_count),
        queries,
        keys_here,
        values_here,
        live_pairs(block_mask, own_start, rows_here, own_start, rows_here),
    )

    def advance(hop_index, cycle_state):
        moving = shifted(shortened(cycle_state[1]), "blk", 1)
        anchor = (own_index - hop_index) % cycle_size
        live_map = live_pairs(block_mask, own_start, rows_here, anchor * rows_here, rows_here)
        return (attend(cycle_state[0], queries, moving[0], moving[1], live_map), moving)

    running, unused = lax.fori_loop(1, cycle_size, advance, (running, (keys_here, values_here)))
    outputs, totals = (running[0], running[2])
    result = (outputs / totals[..., None]).astype(jnp.bfloat16).reshape(rows_here, head_count * HD)
    return lax.all_to_all(result, "head", split_axis=0, concat_axis=1, tiled=True)


def solution(mesh):
    return jax.shard_map(
        on_device,
        mesh=mesh,
        in_specs=(P(("blk", "head"), None), P()),
        out_specs=P(("blk", "head"), None),
        check_vma=False,
    )
```

profile of v0, /device:TPU:128, one launch (start us, length us, event | category | flops | bytes accessed | tf_op | source)
XLA Modules:
  0.0 193.9 jit_solution(1147149548985235752)
XLA Ops:
  0.0 2.1 %copy.69 = bf16[4,32,8,384]{3,2,0,1:T(8,128)(2,1)} copy(bf16[4,32,8,384]{3,2,1,0:T(8,128)(2,1)} %bitcast.295) | data formatting | bytes 1572864 | tf_op jit(solution)/shard_map/all_to_all | solution.py:80
  2.1 7.8 %all-to-all-start = ((bf16[32,32,384]{2,0,1:T(8,128)(2,1)}), bf16[32,32,384]{2,0,1:T(8,128)(2,1)S(1)}, u32[]{:S(2)}, u32[]{:S(2)}) async-start(bf16[32,32,384]{2,0,1:T(8,128)(2,1)} %bitcast.228), calls=%async_computation | async-start | bytes 1572864 | tf_op jit(solution)/shard_map/all_to_all | solution.py:80
  11.1 1.3 bitcast_or_fusion.1
  12.4 11.2 %all-to-all-done = bf16[32,32,384]{2,0,1:T(8,128)(2,1)S(1)} async-done(((bf16[32,32,384]{2,0,1:T(8,128)(2,1)}), bf16[32,32,384]{2,0,1:T(8,128)(2,1)S(1)}, u32[]{:S(2)}, u32[]{:S(2)}) %all-to-all-start) | async-done | bytes 786464 | tf_op jit(solution)/shard_map/all_to_all | solution.py:80
  23.8 0.9 fusion.85
  24.8 1.1 fusion.84
  26.5 1.2 fusion.37
  27.7 1.0 convolution_bitcast_fusion.2
  28.7 1.6 fusion.39
  30.4 1.1 fusion.46
  31.5 139.9 %while.24 = (s32[]{:T(128)}, f32[1024,1,128]{2,0,1:T(8,128)S(1)}, f32[1024,1]{0,1:T(1,128)S(1)}, f32[1024,1]{0,1:T(1,128)S(1)}, bf16[1024,1,128]{2,0,1:T(8,128)(...) while((s32[]{:T(128)}, f32[1024,1,128]{2,0,1:T(8,128)S(1)}, ...), condition=%wide.region_9.10_spmd, body=%wide.region_4.9_spmd.sunk | while | flops 553160832 | bytes 27387844 | solution.py:104
  31.8 1.6 collective-permute-start
  34.6 1.3 bitcast_or_fusion.3
  35.9 12.0 %collective-permute-done = bf16[1024,1,128]{2,0,1:T(8,128)(2,1)S(1)} collective-permute-done((bf16[1024,1,128]{2,0,1:T(8,128)(2,1)S(1)}, bf16[1024,1,128]{2,0,1:T(8,128)(2,1)S(1)}, u32[]{:S(2)}, u32[]{:S(2)}) %collective-permute-start) | collective-permute-done | bytes 262176 | tf_op jit(solution)/shard_map/while/body/eval_jaxpr/ppermute | solution.py:23
  48.3 1.2 fusion.99
  49.5 1.6 fusion.101
  52.2 1.3 fusion.102
  54.9 1.3 bitcast_or_fusion.3
  56.2 13.6 %collective-permute-done = bf16[1024,1,128]{2,0,1:T(8,128)(2,1)S(1)} collective-permute-done((bf16[1024,1,128]{2,0,1:T(8,128)(2,1)S(1)}, bf16[1024,1,128]{2,0,1:T(8,128)(2,1)S(1)}, u32[]{:S(2)}, u32[]{:S(2)}) %collective-permute-start) | collective-permute-done | bytes 262176 | tf_op jit(solution)/shard_map/while/body/eval_jaxpr/ppermute | solution.py:23
  70.2 1.2 fusion.99
  71.5 1.6 fusion.101
  74.2 1.3 fusion.102
  76.9 1.3 bitcast_or_fusion.3
  78.2 8.9 %collective-permute-done = bf16[1024,1,128]{2,0,1:T(8,128)(2,1)S(1)} collective-permute-done((bf16[1024,1,128]{2,0,1:T(8,128)(2,1)S(1)}, bf16[1024,1,128]{2,0,1:T(8,128)(2,1)S(1)}, u32[]{:S(2)}, u32[]{:S(2)}) %collective-permute-start) | collective-permute-done | bytes 262176 | tf_op jit(solution)/shard_map/while/body/eval_jaxpr/ppermute | solution.py:23
  87.5 1.2 fusion.99
  88.7 1.6 fusion.101
  91.4 1.3 fusion.102
  94.2 1.3 bitcast_or_fusion.3
  95.5 11.0 %collective-permute-done = bf16[1024,1,128]{2,0,1:T(8,128)(2,1)S(1)} collective-permute-done((bf16[1024,1,128]{2,0,1:T(8,128)(2,1)S(1)}, bf16[1024,1,128]{2,0,1:T(8,128)(2,1)S(1)}, u32[]{:S(2)}, u32[]{:S(2)}) %collective-permute-start) | collective-permute-done | bytes 262176 | tf_op jit(solution)/shard_map/while/body/eval_jaxpr/ppermute | solution.py:23
  106.9 1.2 fusion.99
  108.1 1.6 fusion.101
  110.8 1.3 fusion.102
  113.5 1.3 bitcast_or_fusion.3
  114.8 13.7 %collective-permute-done = bf16[1024,1,128]{2,0,1:T(8,128)(2,1)S(1)} collective-permute-done((bf16[1024,1,128]{2,0,1:T(8,128)(2,1)S(1)}, bf16[1024,1,128]{2,0,1:T(8,128)(2,1)S(1)}, u32[]{:S(2)}, u32[]{:S(2)}) %collective-permute-start) | collective-permute-done | bytes 262176 | tf_op jit(solution)/shard_map/while/body/eval_jaxpr/ppermute | solution.py:23
  128.9 1.2 fusion.99
  130.1 1.6 fusion.101
  132.8 1.3 fusion.102
  135.6 1.3 bitcast_or_fusion.3
  136.9 9.6 %collective-permute-done = bf16[1024,1,128]{2,0,1:T(8,128)(2,1)S(1)} collective-permute-done((bf16[1024,1,128]{2,0,1:T(8,128)(2,1)S(1)}, bf16[1024,1,128]{2,0,1:T(8,128)(2,1)S(1)}, u32[]{:S(2)}, u32[]{:S(2)}) %collective-permute-start) | collective-permute-done | bytes 262176 | tf_op jit(solution)/shard_map/while/body/eval_jaxpr/ppermute | solution.py:23
  146.8 1.2 fusion.99
  148.1 1.6 fusion.101
  150.8 1.3 fusion.102
  153.5 1.3 bitcast_or_fusion.3
  154.8 11.0 %collective-permute-done = bf16[1024,1,128]{2,0,1:T(8,128)(2,1)S(1)} collective-permute-done((bf16[1024,1,128]{2,0,1:T(8,128)(2,1)S(1)}, bf16[1024,1,128]{2,0,1:T(8,128)(2,1)S(1)}, u32[]{:S(2)}, u32[]{:S(2)}) %collective-permute-start) | collective-permute-done | bytes 262176 | tf_op jit(solution)/shard_map/while/body/eval_jaxpr/ppermute | solution.py:23
  166.2 1.2 fusion.99
  167.4 1.6 fusion.101
  170.1 1.3 fusion.102
  171.6 21.6 %all_to_all.35 = bf16[32,32,128]{2,1,0:T(8,128)(2,1)S(1)} all-to-all(bf16[32,32,128]{2,1,0:T(8,128)(2,1)S(1)} %bitcast.292), channel_id=1, replica_groups=mesh['blk'=8,'head'=32] {'head'}, dimensions={0} | all-to-all | bytes 524288 | tf_op jit(solution)/shard_map/all_to_all | solution.py:107
  (116 shorter events, 22.7 us)
Async XLA Ops:
  2.1 21.5 %all-to-all-start = ((bf16[32,32,384]{2,0,1:T(8,128)(2,1)}), bf16[32,32,384]{2,0,1:T(8,128)(2,1)S(1)}, u32[]{:S(2)}, u32[]{:S(2)}) async-start(bf16[32,32,384]{2,0,1:T(8,128)(2,1)} %bitcast.228), calls=%async_computation | async-start | bytes 1572864 | tf_op jit(solution)/shard_map/all_to_all | solution.py:80
  31.7 19.5 %collective-permute-start.1 = (bf16[1024,1,128]{2,0,1:T(8,128)(2,1)S(1)}, bf16[1024,1,128]{2,0,1:T(8,128)(2,1)S(1)}, u32[]{:S(2)}, u32[]{:S(2)}) collective-permute-start(bf16[1024,1,128]{2,0,1:T(8,128)(2,1)S(1)} %get-tuple-element.579), channel_id=1, source_target_pairs={{0,32},{32,64},{64,96},{96,128},{128,160},{160,192},{192,224},{224... | collective-permute-start | bytes 786440 | tf_op jit(solution)/shard_map/while/body/eval_jaxpr/ppermute | solution.py:23
  31.8 16.1 %collective-permute-start = (bf16[1024,1,128]{2,0,1:T(8,128)(2,1)S(1)}, bf16[1024,1,128]{2,0,1:T(8,128)(2,1)S(1)}, u32[]{:S(2)}, u32[]{:S(2)}) collective-permute-start(bf16[1024,1,128]{2,0,1:T(8,128)(2,1)S(1)} %get-tuple-element.578), channel_id=1, source_target_pairs={{0,32},{32,64},{64,96},{96,128},{128,160},{160,192},{192,224},{224... | collective-permute-start | bytes 786440 | tf_op jit(solution)/shard_map/while/body/eval_jaxpr/ppermute | solution.py:23
  53.5 19.7 %collective-permute-start.1 = (bf16[1024,1,128]{2,0,1:T(8,128)(2,1)S(1)}, bf16[1024,1,128]{2,0,1:T(8,128)(2,1)S(1)}, u32[]{:S(2)}, u32[]{:S(2)}) collective-permute-start(bf16[1024,1,128]{2,0,1:T(8,128)(2,1)S(1)} %get-tuple-element.579), channel_id=1, source_target_pairs={{0,32},{32,64},{64,96},{96,128},{128,160},{160,192},{192,224},{224... | collective-permute-start | bytes 786440 | tf_op jit(solution)/shard_map/while/body/eval_jaxpr/ppermute | solution.py:23
  53.6 16.2 %collective-permute-start = (bf16[1024,1,128]{2,0,1:T(8,128)(2,1)S(1)}, bf16[1024,1,128]{2,0,1:T(8,128)(2,1)S(1)}, u32[]{:S(2)}, u32[]{:S(2)}) collective-permute-start(bf16[1024,1,128]{2,0,1:T(8,128)(2,1)S(1)} %get-tuple-element.578), channel_id=1, source_target_pairs={{0,32},{32,64},{64,96},{96,128},{128,160},{160,192},{192,224},{224... | collective-permute-start | bytes 786440 | tf_op jit(solution)/shard_map/while/body/eval_jaxpr/ppermute | solution.py:23
  75.4 15.0 %collective-permute-start.1 = (bf16[1024,1,128]{2,0,1:T(8,128)(2,1)S(1)}, bf16[1024,1,128]{2,0,1:T(8,128)(2,1)S(1)}, u32[]{:S(2)}, u32[]{:S(2)}) collective-permute-start(bf16[1024,1,128]{2,0,1:T(8,128)(2,1)S(1)} %get-tuple-element.579), channel_id=1, source_target_pairs={{0,32},{32,64},{64,96},{96,128},{128,160},{160,192},{192,224},{224... | collective-permute-start | bytes 786440 | tf_op jit(solution)/shard_map/while/body/eval_jaxpr/ppermute | solution.py:23
  75.5 11.5 %collective-permute-start = (bf16[1024,1,128]{2,0,1:T(8,128)(2,1)S(1)}, bf16[1024,1,128]{2,0,1:T(8,128)(2,1)S(1)}, u32[]{:S(2)}, u32[]{:S(2)}) collective-permute-start(bf16[1024,1,128]{2,0,1:T(8,128)(2,1)S(1)} %get-tuple-element.578), channel_id=1, source_target_pairs={{0,32},{32,64},{64,96},{96,128},{128,160},{160,192},{192,224},{224... | collective-permute-start | bytes 786440 | tf_op jit(solution)/shard_map/while/body/eval_jaxpr/ppermute | solution.py:23
  92.7 17.1 %collective-permute-start.1 = (bf16[1024,1,128]{2,0,1:T(8,128)(2,1)S(1)}, bf16[1024,1,128]{2,0,1:T(8,128)(2,1)S(1)}, u32[]{:S(2)}, u32[]{:S(2)}) collective-permute-start(bf16[1024,1,128]{2,0,1:T(8,128)(2,1)S(1)} %get-tuple-element.579), channel_id=1, source_target_pairs={{0,32},{32,64},{64,96},{96,128},{128,160},{160,192},{192,224},{224... | collective-permute-start | bytes 786440 | tf_op jit(solution)/shard_map/while/body/eval_jaxpr/ppermute | solution.py:23
  92.8 13.6 %collective-permute-start = (bf16[1024,1,128]{2,0,1:T(8,128)(2,1)S(1)}, bf16[1024,1,128]{2,0,1:T(8,128)(2,1)S(1)}, u32[]{:S(2)}, u32[]{:S(2)}) collective-permute-start(bf16[1024,1,128]{2,0,1:T(8,128)(2,1)S(1)} %get-tuple-element.578), channel_id=1, source_target_pairs={{0,32},{32,64},{64,96},{96,128},{128,160},{160,192},{192,224},{224... | collective-permute-start | bytes 786440 | tf_op jit(solution)/shard_map/while/body/eval_jaxpr/ppermute | solution.py:23
  112.1 19.8 %collective-permute-start.1 = (bf16[1024,1,128]{2,0,1:T(8,128)(2,1)S(1)}, bf16[1024,1,128]{2,0,1:T(8,128)(2,1)S(1)}, u32[]{:S(2)}, u32[]{:S(2)}) collective-permute-start(bf16[1024,1,128]{2,0,1:T(8,128)(2,1)S(1)} %get-tuple-element.579), channel_id=1, source_target_pairs={{0,32},{32,64},{64,96},{96,128},{128,160},{160,192},{192,224},{224... | collective-permute-start | bytes 786440 | tf_op jit(solution)/shard_map/while/body/eval_jaxpr/ppermute | solution.py:23
  112.2 16.3 %collective-permute-start = (bf16[1024,1,128]{2,0,1:T(8,128)(2,1)S(1)}, bf16[1024,1,128]{2,0,1:T(8,128)(2,1)S(1)}, u32[]{:S(2)}, u32[]{:S(2)}) collective-permute-start(bf16[1024,1,128]{2,0,1:T(8,128)(2,1)S(1)} %get-tuple-element.578), channel_id=1, source_target_pairs={{0,32},{32,64},{64,96},{96,128},{128,160},{160,192},{192,224},{224... | collective-permute-start | bytes 786440 | tf_op jit(solution)/shard_map/while/body/eval_jaxpr/ppermute | solution.py:23
  134.1 15.7 %collective-permute-start.1 = (bf16[1024,1,128]{2,0,1:T(8,128)(2,1)S(1)}, bf16[1024,1,128]{2,0,1:T(8,128)(2,1)S(1)}, u32[]{:S(2)}, u32[]{:S(2)}) collective-permute-start(bf16[1024,1,128]{2,0,1:T(8,128)(2,1)S(1)} %get-tuple-element.579), channel_id=1, source_target_pairs={{0,32},{32,64},{64,96},{96,128},{128,160},{160,192},{192,224},{224... | collective-permute-start | bytes 786440 | tf_op jit(solution)/shard_map/while/body/eval_jaxpr/ppermute | solution.py:23
  134.2 12.2 %collective-permute-start = (bf16[1024,1,128]{2,0,1:T(8,128)(2,1)S(1)}, bf16[1024,1,128]{2,0,1:T(8,128)(2,1)S(1)}, u32[]{:S(2)}, u32[]{:S(2)}) collective-permute-start(bf16[1024,1,128]{2,0,1:T(8,128)(2,1)S(1)} %get-tuple-element.578), channel_id=1, source_target_pairs={{0,32},{32,64},{64,96},{96,128},{128,160},{160,192},{192,224},{224... | collective-permute-start | bytes 786440 | tf_op jit(solution)/shard_map/while/body/eval_jaxpr/ppermute | solution.py:23
  152.1 17.1 %collective-permute-start.1 = (bf16[1024,1,128]{2,0,1:T(8,128)(2,1)S(1)}, bf16[1024,1,128]{2,0,1:T(8,128)(2,1)S(1)}, u32[]{:S(2)}, u32[]{:S(2)}) collective-permute-start(bf16[1024,1,128]{2,0,1:T(8,128)(2,1)S(1)} %get-tuple-element.579), channel_id=1, source_target_pairs={{0,32},{32,64},{64,96},{96,128},{128,160},{160,192},{192,224},{224... | collective-permute-start | bytes 786440 | tf_op jit(solution)/shard_map/while/body/eval_jaxpr/ppermute | solution.py:23
  152.1 13.6 %collective-permute-start = (bf16[1024,1,128]{2,0,1:T(8,128)(2,1)S(1)}, bf16[1024,1,128]{2,0,1:T(8,128)(2,1)S(1)}, u32[]{:S(2)}, u32[]{:S(2)}) collective-permute-start(bf16[1024,1,128]{2,0,1:T(8,128)(2,1)S(1)} %get-tuple-element.578), channel_id=1, source_target_pairs={{0,32},{32,64},{64,96},{96,128},{128,160},{160,192},{192,224},{224... | collective-permute-start | bytes 786440 | tf_op jit(solution)/shard_map/while/body/eval_jaxpr/ppermute | solution.py:23
where the time goes:
time: 195 us; the launch traced here: 194 us
  waiting for transfers between devices  90.8 us (47%)
  matrix products  30.6 us (16%)
  other arithmetic  24.9 us (13%)
  blocking collectives  21.6 us (11%)
  local copies, waits for them, and re-layouts  14.3 us (7%)
  starting transfers between devices  10.5 us (5%)
    ppermute x14, waiting for transfers between devices, shifted(): return lax.ppermute(x, axis, [(i, (i + by) % size) for i in range(size)])  79.6 us
    all_to_all x1, blocking collectives, on_device(): lax.all_to_all(result, 'head', split_axis=0, concat_axis=1, tiled=True)  21.6 us
    dot_general x16, matrix products, attend(): jnp.einsum('qhk,khd->qhd', weights.astype(jnp.bfloat16), values_part[offs...  17.5 us
    reduce_sum x8, other arithmetic, attend(): totals = totals * factor + jnp.sum(weights, axis=-1)  13.1 us
    dot_general x16, matrix products, attend(): jnp.einsum('qhd,khd->qhk', queries, keys_part[offset:offset + stride], pr...  13 us
    all_to_all x1, waiting for transfers between devices, on_device(): lax.all_to_all(tokens_qkv, 'head', split_axis=1, concat_axis=0, tiled=True)  11.2 us
    or x8, other arithmetic, live_pairs(): return spread | (row_blocks[:, None] == col_blocks[None, :])  10.3 us
    all_to_all x1, starting transfers between devices, on_device(): lax.all_to_all(tokens_qkv, 'head', split_axis=1, concat_axis=0, tiled=True)  7.78 us
  transfers between devices with their start and end apart: 15, of which 8 were waited for; matrix products, arithmetic and copies ran while one was open for 22% of the time, Pallas kernels for 0%

commit v1 on v0

v1 whole, which is shorter than its diff:
```python
import functools
import math

import jax
import jax.numpy as jnp
from jax import lax
from jax.experimental import pallas as pl
from jax.experimental.pallas import tpu as pltpu
from jax.sharding import PartitionSpec as P

MESH = pl.DeviceIdType.MESH
HD = 128
BLOCK = 128
ROWS = 32
NX, NY, NZ, NC = 4, 4, 8, 2
QUERIES = NY * NZ * ROWS
CHUNK = NX * NC * NY * ROWS
TILE = 256
NEGATIVE = -1e30
EXPONENT = math.log2(math.e) / math.sqrt(HD)


def device_at(x, y, z, c):
    return ((z // 2) * NC + c, y * 8 + (z % 2) * NX + x)


def z_offset(i):
    return ((i + 1) // 2) * (2 * (i % 2) - 1)


def block_of(y, z, c):
    return ((z // 2) * NC + c) * 8 + y * 2 + z % 2


def kernel(
    tokens, mask, out, kv, qa, acc, top, bias, result,
    q_sem, kv_sem, own_send, ring_sem, ring_send, out_sem, out_send,
):
    blk, place = lax.axis_index("blk"), lax.axis_index("head")
    c, y, x = blk % NC, place // 8, place % NX
    z = (blk // NC) * 2 + (place // NX) % 2
    head = y * NZ + z
    right, left, across = (x + 1) % NX, (x + NX - 1) % NX, (x + 2) % NX
    other = 1 - c

    barrier = pltpu.get_barrier_semaphore()

    def peer(t):
        return (y + t % NY) % NY, (z + z_offset(t // NY) + NZ) % NZ

    @pl.loop(1, NY * NZ)
    def _(t):
        py, pz = peer(t)
        pl.semaphore_signal(barrier, inc=1, device_id=device_at(x, py, pz, c), device_id_type=MESH)

    for where in (device_at(left, y, z, c), device_at(right, y, z, c), device_at(x, y, z, other)):
        pl.semaphore_signal(barrier, inc=1, device_id=where, device_id_type=MESH)
    pl.semaphore_wait(barrier, NY * NZ + 2)

    my_rows = pl.ds(pl.multiple_of(y * ROWS, ROWS), ROWS)

    def send_kv(t):
        py, pz = peer(t)
        columns = pl.ds(pl.multiple_of((py * NZ + pz) * 3 * HD + HD, HD), 2 * HD)
        pltpu.make_async_remote_copy(
            src_ref=tokens.at[:, columns],
            dst_ref=kv.at[z, x, c, my_rows, :],
            send_sem=own_send.at[0],
            recv_sem=kv_sem.at[z],
            device_id=device_at(x, py, pz, c),
            device_id_type=MESH,
        ).start()

    def send_q(t):
        py, pz = peer(t)
        columns = pl.ds(pl.multiple_of((py * NZ + pz) * 3 * HD, HD), HD)
        pltpu.make_async_remote_copy(
            src_ref=tokens.at[:, columns],
            dst_ref=qa.at[pl.ds(pl.multiple_of((z * NY + y) * ROWS, ROWS), ROWS), pl.ds(0, HD)],
            send_sem=own_send.at[1],
            recv_sem=q_sem.at[0],
            device_id=device_at(x, py, pz, c),
            device_id_type=MESH,
        ).start()

    pltpu.make_async_copy(
        tokens.at[:, pl.ds(pl.multiple_of(head * 3 * HD + HD, HD), 2 * HD)], kv.at[z, x, c, my_rows, :], kv_sem.at[z]
    ).start()
    pltpu.make_async_copy(
        tokens.at[:, pl.ds(pl.multiple_of(head * 3 * HD, HD), HD)],
        qa.at[pl.ds(pl.multiple_of((z * NY + y) * ROWS, ROWS), ROWS), pl.ds(0, HD)],
        q_sem.at[0],
    ).start()
    pl.loop(1, NY)(send_kv)
    pl.loop(1, NY * NZ)(send_q)
    pl.loop(NY, NY * NZ)(send_kv)

    row_block = lax.broadcasted_iota(jnp.int32, (64, 64), 0)
    col_block = lax.broadcasted_iota(jnp.int32, (64, 64), 1)
    bias[...] = jnp.zeros_like(bias)
    bias[:, 0:64] = jnp.where((mask[...] == 1) | (row_block == col_block), 0.0, NEGATIVE)

    @pl.loop(0, NY * NZ)
    def _(g):
        line = bias[pl.ds(block_of(g % NY, g // NY, c), 1), :]
        rows = pl.ds(pl.multiple_of(g * ROWS, ROWS), ROWS)
        qa[rows, HD : 2 * HD] = jnp.broadcast_to(line, (ROWS, HD)).astype(jnp.bfloat16)

    acc[...] = jnp.zeros_like(acc)
    top[...] = jnp.full_like(top, NEGATIVE)

    def chunk_of(s):
        return (z + NZ - z_offset(s)) % NZ

    def ring(zc, xc, where, send):
        return pltpu.make_async_remote_copy(
            src_ref=kv.at[zc, xc, c],
            dst_ref=kv.at[zc, xc, c],
            send_sem=ring_send.at[send],
            recv_sem=ring_sem.at[zc, xc, c],
            device_id=where,
            device_id_type=MESH,
        )

    def arrived(zc, xc, cc):
        pltpu.make_async_copy(kv.at[zc, xc, cc], kv.at[zc, xc, cc], ring_sem.at[zc, xc, cc]).wait()

    at_right, at_left, at_other = device_at(right, y, z, c), device_at(left, y, z, c), device_at(x, y, z, other)

    def send_tile(j):
        @pl.loop(0, TILE // ROWS)
        def _(g):
            group = j * (TILE // ROWS) + g
            py, pz = group % NY, group // NY
            source = result.at[pl.ds(pl.multiple_of(group * ROWS, ROWS), ROWS), :]
            target = out.at[:, pl.ds(pl.multiple_of(head * HD, HD), HD)]
            mine = (py == y) & (pz == z)

            @pl.when(mine)
            def _():
                pltpu.make_async_copy(source, target, out_sem.at[0]).start()

            @pl.when(jnp.logical_not(mine))
            def _():
                pltpu.make_async_remote_copy(
                    src_ref=source, dst_ref=target, send_sem=out_send.at[0], recv_sem=out_sem.at[0],
                    device_id=device_at(x, py, pz, c), device_id_type=MESH,
                ).start()

    def attend(zc, last):
        row = lax.broadcasted_iota(jnp.int32, (NC * NY * ROWS, HD), 0)
        col = lax.broadcasted_iota(jnp.int32, (NC * NY * ROWS, HD), 1)
        first = (zc // 2) * NC * 8 + zc % 2
        hot = (col == first + (row // (NY * ROWS)) * 8 + ((row // ROWS) % NY) * 2)
        hot = jnp.where(hot, 1.0, 0.0).astype(jnp.bfloat16)
        hot = jnp.concatenate([hot] * NX, axis=0)
        keys = jnp.concatenate([kv[zc, :, :, :, 0:HD].reshape(CHUNK, HD), hot], axis=1)
        values = jnp.concatenate(
            [kv[zc, :, :, :, HD : 2 * HD].reshape(CHUNK, HD), jnp.ones((CHUNK, HD), jnp.bfloat16)], axis=1
        )

        for j in range(QUERIES // TILE):
            rows = slice(j * TILE, (j + 1) * TILE)
            scores = lax.dot_general(
                qa[rows, :], keys, (((1,), (1,)), ((), ())), preferred_element_type=jnp.float32
            )
            old = top[rows, :]
            new = jnp.maximum(old, jnp.max(scores, axis=1, keepdims=True))
            top[rows, :] = new
            weights = jnp.exp2((scores - new[:, 0:1]) * EXPONENT).astype(jnp.bfloat16)
            factor = jnp.exp2((old - new) * EXPONENT)
            acc[rows, :] = acc[rows, :] * jnp.concatenate([factor, factor], axis=1) + jnp.dot(
                weights, values, preferred_element_type=jnp.float32
            )

    @pl.loop(0, NZ + 3)
    def _(s):
        @pl.when(s < NZ)
        def _():
            zc = chunk_of(s)
            pltpu.make_async_copy(kv.at[zc, x, c], kv.at[zc, x, c], kv_sem.at[zc]).wait()
            ring(zc, x, at_right, 0).start()
            ring(zc, x, at_left, 1).start()
            ring(zc, x, at_other, 2).start()

        @pl.when((s >= 1) & (s <= NZ))
        def _():
            zc = chunk_of(s - 1)
            arrived(zc, left, c)
            arrived(zc, right, c)

            @pl.when(s % 2 == 0)
            def _():
                ring(zc, left, at_right, 3).start()

            @pl.when(s % 2 == 1)
            def _():
                ring(zc, right, at_left, 3).start()

            ring(zc, left, at_other, 4).start()
            ring(zc, right, at_other, 5).start()

        @pl.when((s >= 2) & (s <= NZ + 1))
        def _():
            zc = chunk_of(s - 2)
            arrived(zc, across, c)
            ring(zc, across, at_other, 6).start()

        @pl.when(s == 3)
        def _():
            pltpu.make_async_copy(qa.at[:, pl.ds(0, HD)], qa.at[:, pl.ds(0, HD)], q_sem.at[0]).wait()

        @pl.when(s >= 3)
        def _():
            zc = chunk_of(s - 3)
            for xc in range(NX):
                arrived(zc, xc, other)
            attend(zc, s == NZ + 2)

    for j in range(QUERIES // TILE):
        rows = slice(j * TILE, (j + 1) * TILE)
        result[rows, :] = (acc[rows, 0:HD] / acc[rows, HD : 2 * HD]).astype(jnp.bfloat16)
        send_tile(j)

    @pl.loop(0, 7)
    def _(i):
        pltpu.make_async_copy(kv.at[:, 0, 0], kv.at[:, 0, 0], ring_send.at[i]).wait()

    sent = pl.ds(0, QUERIES - ROWS)
    pltpu.make_async_copy(qa.at[sent, :], qa.at[sent, :], own_send.at[0]).wait()
    pltpu.make_async_copy(result.at[sent, :], result.at[sent, :], own_send.at[1]).wait()
    pltpu.make_async_copy(result.at[sent, :], result.at[sent, :], out_send.at[0]).wait()
    pltpu.make_async_copy(result, result, out_sem.at[0]).wait()


def on_device(tokens_qkv, block_mask):
    dma = pltpu.SemaphoreType.DMA
    return pl.pallas_call(
        kernel,
        out_shape=jax.ShapeDtypeStruct((ROWS, NY * NZ * HD), jnp.bfloat16),
        in_specs=[pl.BlockSpec(memory_space=pl.ANY), pl.BlockSpec(memory_space=pltpu.VMEM)],
        out_specs=pl.BlockSpec(memory_space=pl.ANY),
        scratch_shapes=[
            pltpu.VMEM((NZ, NX, NC, NY * ROWS, 2 * HD), jnp.bfloat16),
            pltpu.VMEM((QUERIES, 2 * HD), jnp.bfloat16),
            pltpu.VMEM((QUERIES, 2 * HD), jnp.float32),
            pltpu.VMEM((QUERIES, HD), jnp.float32),
            pltpu.VMEM((64, HD), jnp.float32),
            pltpu.VMEM((QUERIES, HD), jnp.bfloat16),
            dma((1,)),
            dma((NZ,)),
            dma((2,)),
            dma((NZ, NX, NC)),
            dma((7,)),
            dma((1,)),
            dma((1,)),
        ],
        compiler_params=pltpu.CompilerParams(
            collective_id=0, has_side_effects=True, vmem_limit_bytes=48 * 1024 * 1024
        ),
        cost_estimate=pl.CostEstimate(flops=8 * 1024 * 8192 * 128, bytes_accessed=1 << 20, transcendentals=1024 * 8192),
    )(tokens_qkv, block_mask)


def solution(mesh):
    return jax.shard_map(
        on_device,
        mesh=mesh,
        in_specs=(P(("blk", "head"), None), P()),
        out_specs=P(("blk", "head"), None),
        check_vma=False,
    )
```

time: 195 us -> 63.5 us (0.33)
  the two profiles are of different devices: /device:TPU:128 before, /device:TPU:1 now
where the time goes in v1:
time: 63.5 us; the launch traced here: 62.3 us
  Pallas kernels  59.7 us (94%)
  local copies, waits for them, and re-layouts  2.6 us (4%)
    pallas_call x1, Pallas kernels, on_device(): pl.pallas_call(kernel, out_shape=jax.ShapeDtypeStruct((ROWS, NY * NZ * HD...  59.7 us
    unnamed x5, local copies, waits for them, and re-layouts  2.6 us

profile of v1, /device:TPU:1, one launch (start us, length us, event | category | flops | bytes accessed | tf_op | source)
XLA Modules:
  0.0 62.3 jit_solution(3880370370815756286)
XLA Ops:
  0.0 0.0 copy-start
  0.0 1.1 %copy-done = bf16[32,12288]{1,0:T(8,128)(2,1)S(1)} copy-done((bf16[32,12288]{1,0:T(8,128)(2,1)S(1)}, bf16[32,12288]{1,0:T(8,128)(2,1)}, u32[]{:S(2)}) %copy-start) | copy-done | bytes 786456
  1.1 0.0 copy-start.1
  1.1 0.8 %copy-done.1 = s32[64,64]{1,0:T(8,128)S(1)} copy-done((s32[64,64]{1,0:T(8,128)S(1)}, s32[64,64]{1,0:T(8,128)}, u32[]{:S(2)}) %copy-start.1) | copy-done | bytes 16408
  1.9 59.7 %shard_map.28 = bf16[32,4096]{1,0:T(8,128)(2,1)S(1)} custom-call(bf16[32,12288]{1,0:T(8,128)(2,1)S(1)} %copy-done, s32[64,64]{1,0:T(8,128)S(1)} %copy-done.1), custom_call_target="tpu_custom_call" | custom-call | flops 8589934592 | bytes 1048576 | tf_op jit(solution)/shard_map/pallas_call | solution.py:238
  61.6 0.7 %copy.4 = bf16[32,4096]{1,0:T(8,128)(2,1)} copy(bf16[32,4096]{1,0:T(8,128)(2,1)S(1)} %shard_map.28) | data formatting | bytes 524288
Async XLA Ops:
  0.0 1.1 %copy-start = (bf16[32,12288]{1,0:T(8,128)(2,1)S(1)}, bf16[32,12288]{1,0:T(8,128)(2,1)}, u32[]{:S(2)}) copy-start(bf16[32,12288]{1,0:T(8,128)(2,1)} %tokens.1) | copy-start | bytes 2359300
  1.1 0.8 %copy-start.1 = (s32[64,64]{1,0:T(8,128)S(1)}, s32[64,64]{1,0:T(8,128)}, u32[]{:S(2)}) copy-start(s32[64,64]{1,0:T(8,128)} %mask.1) | copy-start | bytes 49156

commit v2 on v1

v2 whole, which is shorter than its diff:
```python
import functools
import math

import jax
import jax.numpy as jnp
from jax import lax
from jax.experimental import pallas as pl
from jax.experimental.pallas import tpu as pltpu
from jax.sharding import PartitionSpec as P

MESH = pl.DeviceIdType.MESH
HD = 128
BLOCK = 128
ROWS = 32
NX, NY, NZ, NC = 4, 4, 8, 2
QUERIES = NY * NZ * ROWS
LINE = NZ * ROWS
PIECE = NX * NC * LINE
TILE = 256
NEGATIVE = -1e30
EXPONENT = math.log2(math.e) / math.sqrt(HD)


def device_at(x, y, z, c):
    return ((z // 2) * NC + c, y * 8 + (z % 2) * NX + x)


def block_of(y, z, c):
    return ((z // 2) * NC + c) * 8 + y * 2 + z % 2


def aligned(start, size):
    return pl.ds(pl.multiple_of(start, size), size)


def kernel(
    tokens, mask, out, held, pairs, stage, kv, qa, acc, top, bias, result,
    in_sem, y_sem, y_send, q_sem, kv_sem, z_send, ring_sem, ring_send, out_sem, out_send,
):
    blk, place = lax.axis_index("blk"), lax.axis_index("head")
    c, y, x = blk % NC, place // 8, place % NX
    z = (blk // NC) * 2 + (place // NX) % 2
    head = y * NZ + z
    right, left, across = (x + 1) % NX, (x + NX - 1) % NX, (x + 2) % NX
    other = 1 - c
    source = (y, (y + 1) % NY, (y + NY - 1) % NY, (y + 2) % NY)
    at_y = (None, device_at(x, source[2], z, c), device_at(x, source[1], z, c), device_at(x, source[3], z, c))
    z_there = [(z + step) % NZ for step in (1, 7, 2, 6, 3, 5, 4)]
    at_z = [device_at(x, y, there, c) for there in z_there]
    at_right, at_left, at_other = device_at(right, y, z, c), device_at(left, y, z, c), device_at(x, y, z, other)

    load = pltpu.make_async_copy(tokens, held, in_sem.at[0])
    load.start()
    load_mask = pltpu.make_async_copy(mask, pairs, in_sem.at[1])
    load_mask.start()

    barrier = pltpu.get_barrier_semaphore()
    for where in [at_other, at_right, at_left] + list(at_y[1:]) + at_z:
        pl.semaphore_signal(barrier, inc=1, device_id=where, device_id_type=MESH)

    load_mask.wait()
    row_block = lax.broadcasted_iota(jnp.int32, (64, 64), 0)
    col_block = lax.broadcasted_iota(jnp.int32, (64, 64), 1)
    bias[...] = jnp.zeros_like(bias)
    bias[:, 0:64] = jnp.where((pairs[...] == 1) | (row_block == col_block), 0.0, NEGATIVE)

    @pl.loop(0, NY * NZ)
    def _(g):
        line = bias[pl.ds(block_of(g // NZ, g % NZ, c), 1), :]
        qa[aligned(g * ROWS, ROWS), HD : 2 * HD] = jnp.broadcast_to(line, (ROWS, HD)).astype(jnp.bfloat16)

    acc[...] = jnp.zeros_like(acc)
    top[...] = jnp.full_like(top, NEGATIVE)
    load.wait()
    pl.semaphore_wait(barrier, NY + NZ + 1)

    wide = NZ * 3 * HD

    def along_y(k):
        pltpu.make_async_remote_copy(
            src_ref=held.at[:, aligned(source[(0, 2, 1, 3)[k]] * wide, wide)],
            dst_ref=stage.at[k - 1],
            send_sem=y_send.at[0],
            recv_sem=y_sem.at[k - 1],
            device_id=at_y[k],
            device_id_type=MESH,
        ).start()

    def from_y(k):
        pltpu.make_async_copy(stage.at[k - 1], stage.at[k - 1], y_sem.at[k - 1]).wait()

    my_rows = aligned(z * ROWS, ROWS)

    def slab(k, there, part):
        width = 2 * HD if part == 0 else HD
        start = there * 3 * HD + (HD if part == 0 else 0)
        if k == 0:
            return held.at[:, pl.ds(pl.multiple_of(y * wide + start, HD), width)]
        return stage.at[k - 1, :, pl.ds(pl.multiple_of(start, HD), width)]

    def landing(k, part):
        if part == 0:
            return kv.at[source[k], x, c, my_rows, :]
        return qa.at[aligned((source[k] * NZ + z) * ROWS, ROWS), pl.ds(0, HD)]

    def along_z(k, part):
        sem = kv_sem.at[k] if part == 0 else q_sem.at[0]
        for i in range(NZ - 1):
            pltpu.make_async_remote_copy(
                src_ref=slab(k, z_there[i], part),
                dst_ref=landing(k, part),
                send_sem=z_send.at[part],
                recv_sem=sem,
                device_id=at_z[i],
                device_id_type=MESH,
            ).start()
        pltpu.make_async_copy(slab(k, z, part), landing(k, part), sem).start()

    def ring(ref, sem, where, send):
        pltpu.make_async_remote_copy(
            src_ref=ref, dst_ref=ref, send_sem=ring_send.at[send], recv_sem=sem, device_id=where, device_id_type=MESH
        ).start()

    def pick(p):
        return lax.rem(y + (p + 1) // 2 * (2 * (p % 2) - 1) + NY, NY)

    def arrived(yp, xc, cc):
        ref = kv.at[yp, xc, cc]
        pltpu.make_async_copy(ref, ref, ring_sem.at[yp, xc, cc]).wait()

    def step_a(p):
        yp = source[p]
        ref = kv.at[yp, x, c]
        pltpu.make_async_copy(ref, ref, kv_sem.at[p]).wait()
        ring(ref, ring_sem.at[yp, x, c], at_right, 0)
        ring(ref, ring_sem.at[yp, x, c], at_left, 1)
        ring(ref, ring_sem.at[yp, x, c], at_other, 2)

    def step_b(p):
        yp = source[p]
        for xc, half, onward, send in ((left, 0, at_right, 3), (right, 1, at_left, 4)):
            arrived(yp, xc, c)
            ring(kv.at[yp, xc, c, pl.ds(half * (LINE // 2), LINE // 2), :], ring_sem.at[yp, xc, c], onward, send)
        ring(kv.at[yp, left, c], ring_sem.at[yp, left, c], at_other, 5)
        ring(kv.at[yp, right, c], ring_sem.at[yp, right, c], at_other, 6)

    def step_c(p):
        yp = source[p]
        arrived(yp, across, c)
        ring(kv.at[yp, across, c], ring_sem.at[yp, across, c], at_other, 7)

    def send_tile(j):
        target = out.at[:, aligned(head * HD, HD)]

        @pl.loop(0, NZ)
        def _(pz):
            piece = result.at[aligned((j * NZ + pz) * ROWS, ROWS), :]
            mine = (j == y) & (pz == z)

            @pl.when(mine)
            def _():
                pltpu.make_async_copy(piece, target, out_sem.at[0]).start()

            @pl.when(jnp.logical_not(mine))
            def _():
                pltpu.make_async_remote_copy(
                    src_ref=piece, dst_ref=target, send_sem=out_send.at[0], recv_sem=out_sem.at[0],
                    device_id=device_at(x, j, pz, c), device_id_type=MESH,
                ).start()

    def attend(yp, start, tiles, finish):
        row = lax.broadcasted_iota(jnp.int32, (NC * LINE, HD), 0)
        col = lax.broadcasted_iota(jnp.int32, (NC * LINE, HD), 1)
        z_row = (row // ROWS) % NZ
        hot = col == block_of(yp, z_row, row // LINE)
        hot = jnp.where(hot, 1.0, 0.0).astype(jnp.bfloat16)
        hot = jnp.concatenate([hot] * NX, axis=0)
        keys = jnp.concatenate([kv[yp, :, :, :, 0:HD].reshape(PIECE, HD), hot], axis=1)
        values = jnp.concatenate(
            [kv[yp, :, :, :, HD : 2 * HD].reshape(PIECE, HD), jnp.ones((PIECE, HD), jnp.bfloat16)], axis=1
        )

        def place_of(j):
            return aligned(start + j * TILE, TILE)

        def score(j):
            return lax.dot_general(
                qa[place_of(j), :], keys, (((1,), (1,)), ((), ())), preferred_element_type=jnp.float32
            )

        ahead = score(0)
        for j in range(tiles):
            rows = place_of(j)
            scores = ahead
            if j + 1 < tiles:
                ahead = score(j + 1)
            old = top[rows, :]
            new = jnp.maximum(old, jnp.max(scores, axis=1, keepdims=True))
            top[rows, :] = new
            weights = jnp.exp2((scores - new[:, 0:1]) * EXPONENT).astype(jnp.bfloat16)
            factor = jnp.exp2((old - new) * EXPONENT)
            total = acc[rows, :] * jnp.concatenate([factor, factor], axis=1) + jnp.dot(
                weights, values, preferred_element_type=jnp.float32
            )
            if finish:
                result[rows, :] = (total[:, 0:HD] / total[:, HD : 2 * HD]).astype(jnp.bfloat16)
                send_tile(j)
            else:
                acc[rows, :] = total

    along_y(1)
    along_y(2)
    along_z(0, 1)
    along_z(0, 0)
    from_y(1)
    along_z(1, 1)
    along_z(1, 0)
    from_y(2)
    along_y(3)
    along_z(2, 1)
    step_a(0)
    from_y(3)
    along_z(3, 1)
    along_z(2, 0)
    along_z(3, 0)
    step_b(0)
    step_a(1)
    step_c(0)
    step_b(1)
    queries = qa.at[:, pl.ds(0, HD)]
    pltpu.make_async_copy(queries, queries, q_sem.at[0]).wait()

    @pl.loop(0, 6)
    def _(i):
        p = i // 2

        @pl.when(i == 2)
        def _():
            step_a(2)
            step_c(1)

        @pl.when(i == 4)
        def _():
            step_a(3)
            step_b(2)
            step_c(2)

        @pl.when(i == 5)
        def _():
            step_b(3)

        @pl.when(i % 2 == 0)
        def _():
            for xc in range(NX):
                arrived(pick(p), xc, other)

        attend(pick(p), (i % 2) * (QUERIES // 2), QUERIES // 2 // TILE, False)

    step_c(3)
    for xc in range(NX):
        arrived(source[3], xc, other)
    attend(source[3], 0, QUERIES // TILE, True)

    def done(ref, sem):
        pltpu.make_async_copy(ref, ref, sem).wait()

    done(stage, y_send.at[0])
    done(qa.at[pl.ds(0, QUERIES - NY * ROWS), :], z_send.at[0])
    done(result.at[pl.ds(0, QUERIES - NY * ROWS), :], z_send.at[1])
    for i in range(8):
        ref = kv.at[:, 0, 0, pl.ds(0, LINE // 2), :] if i in (3, 4) else kv.at[:, 0, 0]
        done(ref, ring_send.at[i])
    done(result.at[pl.ds(0, QUERIES - ROWS), :], out_send.at[0])
    done(result, out_sem.at[0])


def on_device(tokens_qkv, block_mask):
    dma = pltpu.SemaphoreType.DMA
    return pl.pallas_call(
        kernel,
        out_shape=jax.ShapeDtypeStruct((ROWS, NY * NZ * HD), jnp.bfloat16),
        in_specs=[pl.BlockSpec(memory_space=pl.ANY), pl.BlockSpec(memory_space=pl.ANY)],
        out_specs=pl.BlockSpec(memory_space=pl.ANY),
        scratch_shapes=[
            pltpu.VMEM((ROWS, NY * NZ * 3 * HD), jnp.bfloat16),
            pltpu.VMEM((64, 64), jnp.int32),
            pltpu.VMEM((NY - 1, ROWS, NZ * 3 * HD), jnp.bfloat16),
            pltpu.VMEM((NY, NX, NC, LINE, 2 * HD), jnp.bfloat16),
            pltpu.VMEM((QUERIES, 2 * HD), jnp.bfloat16),
            pltpu.VMEM((QUERIES, 2 * HD), jnp.float32),
            pltpu.VMEM((QUERIES, HD), jnp.float32),
            pltpu.VMEM((64, HD), jnp.float32),
            pltpu.VMEM((QUERIES, HD), jnp.bfloat16),
            dma((2,)),
            dma((NY - 1,)),
            dma((1,)),
            dma((1,)),
            dma((NY,)),
            dma((2,)),
            dma((NY, NX, NC)),
            dma((8,)),
            dma((1,)),
            dma((1,)),
        ],
        compiler_params=pltpu.CompilerParams(
            collective_id=0, has_side_effects=True, vmem_limit_bytes=62 * 1024 * 1024
        ),
        cost_estimate=pl.CostEstimate(flops=8 * 1024 * 8192 * 128, bytes_accessed=1 << 20, transcendentals=1024 * 8192),
    )(tokens_qkv, block_mask)


def solution(mesh):
    return jax.shard_map(
        on_device,
        mesh=mesh,
        in_specs=(P(("blk", "head"), None), P()),
        out_specs=P(("blk", "head"), None),
        check_vma=False,
    )
```

time: 63.5 us -> 61.7 us (0.972)
  the two profiles are of different devices: /device:TPU:1 before, /device:TPU:25 now
where the time goes in v2:
time: 61.7 us; the launch traced here: 61.6 us
  Pallas kernels  59.9 us (97%)
  local copies, waits for them, and re-layouts  1.67 us (3%)
    pallas_call x1, Pallas kernels, on_device(): pl.pallas_call(kernel, out_shape=jax.ShapeDtypeStruct((ROWS, NY * NZ * HD...  59.9 us
    unnamed x1, local copies, waits for them, and re-layouts  1.67 us

profile of v2, /device:TPU:25, one launch (start us, length us, event | category | flops | bytes accessed | tf_op | source)
XLA Modules:
  0.0 61.6 jit_solution(17460517749595510206)
XLA Ops:
  0.0 59.9 %shard_map.28 = bf16[32,4096]{1,0:T(8,128)(2,1)} custom-call(bf16[32,12288]{1,0:T(8,128)(2,1)} %tokens.1, s32[64,64]{1,0:T(8,128)} %mask.1), custom_call_target="tpu_custom_call" | custom-call | flops 8589934592 | bytes 1048576 | tf_op jit(solution)/shard_map/pallas_call | solution.py:279
  59.9 1.7 %copy.4 = bf16[32,4096]{1,0:T(8,128)(2,1)} copy(bf16[32,4096]{1,0:T(8,128)(2,1)} %shard_map.28) | data formatting | bytes 524288

commit v3 on v2

v3 whole, which is shorter than its diff:
```python
import functools
import math

import jax
import jax.numpy as jnp
from jax import lax
from jax.experimental import pallas as pl
from jax.experimental.pallas import tpu as pltpu
from jax.sharding import PartitionSpec as P

MESH = pl.DeviceIdType.MESH
HD = 128
BLOCK = 128
ROWS = 32
NX, NY, NZ, NC = 4, 4, 8, 2
QUERIES = NY * NZ * ROWS
HALF = ROWS // 2
LINE = NZ * HALF
PIECE = 2 * NX * NC * LINE
TILE = 256
NEGATIVE = -1e30
EXPONENT = math.log2(math.e) / math.sqrt(HD)


BEFORE = (
    "Y1Y2K0Q0y1y2A0W1K1w1Q1W2K2Y3y3w2",
    "Q2W3K3w3Q3A1A2A3B0B1A4A5B2B3C0C1",
)
STEPS = ("A6S0R0R1", "A7B4B5C2C3S1", "B6R2R3", "B7C4C5", "C6S2", "C7")
AFTER = "S3"


def device_at(x, y, z, c):
    return ((z // 2) * NC + c, y * 8 + (z % 2) * NX + x)


def block_of(y, z, c):
    return ((z // 2) * NC + c) * 8 + y * 2 + z % 2


def aligned(start, size):
    return pl.ds(pl.multiple_of(start, size), size)


def kernel(
    tokens, mask, out, held, pairs, stage, kv, qa, acc, top, bias, result,
    in_sem, y_sem, y_send, q_sem, kv_sem, z_send, ring_sem, ring_send, out_sem, out_send,
):
    blk, place = lax.axis_index("blk"), lax.axis_index("head")
    c, y, x = blk % NC, place // 8, place % NX
    z = (blk // NC) * 2 + (place // NX) % 2
    head = y * NZ + z
    right, left, across = (x + 1) % NX, (x + NX - 1) % NX, (x + 2) % NX
    other = 1 - c
    source = (y, (y + 1) % NY, (y + NY - 1) % NY, (y + 2) % NY)
    at_y = (None, device_at(x, source[2], z, c), device_at(x, source[1], z, c), device_at(x, source[3], z, c))
    z_there = [(z + step) % NZ for step in (1, 7, 2, 6, 3, 5, 4)]
    at_z = [device_at(x, y, there, c) for there in z_there]
    at_right, at_left, at_other = device_at(right, y, z, c), device_at(left, y, z, c), device_at(x, y, z, other)

    load = pltpu.make_async_copy(tokens, held, in_sem.at[0])
    load.start()
    load_mask = pltpu.make_async_copy(mask, pairs, in_sem.at[1])
    load_mask.start()

    barrier = pltpu.get_barrier_semaphore()
    for where in [at_other, at_right, at_left] + list(at_y[1:]) + at_z:
        pl.semaphore_signal(barrier, inc=1, device_id=where, device_id_type=MESH)

    load_mask.wait()
    row_block = lax.broadcasted_iota(jnp.int32, (64, 64), 0)
    col_block = lax.broadcasted_iota(jnp.int32, (64, 64), 1)
    bias[...] = jnp.zeros_like(bias)
    bias[:, 0:64] = jnp.where((pairs[...] == 1) | (row_block == col_block), 0.0, NEGATIVE)

    @pl.loop(0, NY * NZ)
    def _(g):
        line = bias[pl.ds(block_of(g // NZ, g % NZ, c), 1), :]
        qa[aligned(g * ROWS, ROWS), HD : 2 * HD] = jnp.broadcast_to(line, (ROWS, HD)).astype(jnp.bfloat16)

    acc[...] = jnp.zeros_like(acc)
    top[...] = jnp.full_like(top, NEGATIVE)
    load.wait()
    pl.semaphore_wait(barrier, NY + NZ + 1)

    wide = NZ * 3 * HD

    def along_y(k, part):
        there = source[(0, 2, 1, 3)[k]]
        for i in range(NZ):
            start = (z_there[i] if i < NZ - 1 else z) * 3 * HD + (HD if part == 0 else 0)
            width = 2 * HD if part == 0 else HD
            pltpu.make_async_remote_copy(
                src_ref=held.at[:, pl.ds(pl.multiple_of(there * wide + start, HD), width)],
                dst_ref=stage.at[k - 1, :, pl.ds(pl.multiple_of(start, HD), width)],
                send_sem=y_send.at[part],
                recv_sem=y_sem.at[k - 1, part],
                device_id=at_y[k],
                device_id_type=MESH,
            ).start()

    def from_y(k, part):
        ref = stage.at[k - 1, :, pl.ds(0, NZ * (HD if part else 2 * HD))]
        pltpu.make_async_copy(ref, ref, y_sem.at[k - 1, part]).wait()

    def slab(k, there, part):
        width = HD if part == 2 else 2 * HD
        start = there * 3 * HD + (0 if part == 2 else HD)
        rows = pl.ds(0, ROWS) if part == 2 else pl.ds(part * HALF, HALF)
        if k == 0:
            return held.at[rows, pl.ds(pl.multiple_of(y * wide + start, HD), width)]
        return stage.at[k - 1, rows, pl.ds(pl.multiple_of(start, HD), width)]

    def landing(k, part):
        if part < 2:
            return kv.at[source[k], part, x, c, aligned(z * HALF, HALF), :]
        return qa.at[aligned((source[k] * NZ + z) * ROWS, ROWS), pl.ds(0, HD)]

    def along_z(k, part):
        sem = kv_sem.at[k, part] if part < 2 else q_sem.at[k]
        for i in range(NZ - 1):
            pltpu.make_async_remote_copy(
                src_ref=slab(k, z_there[i], part),
                dst_ref=landing(k, part),
                send_sem=z_send.at[part // 2],
                recv_sem=sem,
                device_id=at_z[i],
                device_id_type=MESH,
            ).start()
        pltpu.make_async_copy(slab(k, z, part), landing(k, part), sem).start()

    def ring(ref, sem, where, send):
        pltpu.make_async_remote_copy(
            src_ref=ref, dst_ref=ref, send_sem=ring_send.at[send], recv_sem=sem, device_id=where, device_id_type=MESH
        ).start()

    def pick(p):
        return lax.rem(y + (p + 1) // 2 * (2 * (p % 2) - 1) + NY, NY)

    def arrived(yp, h, xc, cc):
        ref = kv.at[yp, h, xc, cc]
        pltpu.make_async_copy(ref, ref, ring_sem.at[yp, h, xc, cc]).wait()

    def step_a(p):
        yp, h = source[p // 2], p % 2
        ref, sem = kv.at[yp, h, x, c], ring_sem.at[yp, h, x, c]
        pltpu.make_async_copy(ref, ref, kv_sem.at[p // 2, h]).wait()
        ring(ref, sem, at_right, 0)
        ring(ref, sem, at_left, 1)
        ring(ref, sem, at_other, 2)

    def step_b(p):
        yp, h = source[p // 2], p % 2
        for xc, half, onward, send in ((left, 0, at_right, 3), (right, 1, at_left, 4)):
            arrived(yp, h, xc, c)
            ring(kv.at[yp, h, xc, c, pl.ds(half * (LINE // 2), LINE // 2), :], ring_sem.at[yp, h, xc, c], onward, send)
        ring(kv.at[yp, h, left, c], ring_sem.at[yp, h, left, c], at_other, 5)
        ring(kv.at[yp, h, right, c], ring_sem.at[yp, h, right, c], at_other, 6)

    def step_c(p):
        yp, h = source[p // 2], p % 2
        arrived(yp, h, across, c)
        ring(kv.at[yp, h, across, c], ring_sem.at[yp, h, across, c], at_other, 7)

    def complete(k):
        for h in range(2):
            for xc in range(NX):
                arrived(source[k], h, xc, other)

    def send_tile(j):
        target = out.at[:, aligned(head * HD, HD)]

        @pl.loop(0, NZ)
        def _(pz):
            piece = result.at[aligned((j * NZ + pz) * ROWS, ROWS), :]
            mine = (j == y) & (pz == z)

            @pl.when(mine)
            def _():
                pltpu.make_async_copy(piece, target, out_sem.at[0]).start()

            @pl.when(jnp.logical_not(mine))
            def _():
                pltpu.make_async_remote_copy(
                    src_ref=piece, dst_ref=target, send_sem=out_send.at[0], recv_sem=out_sem.at[0],
                    device_id=device_at(x, j, pz, c), device_id_type=MESH,
                ).start()

    def attend(k, half, finish):
        yp = pick(k)
        row = lax.broadcasted_iota(jnp.int32, (NC * LINE, HD), 0)
        col = lax.broadcasted_iota(jnp.int32, (NC * LINE, HD), 1)
        hot = col == block_of(yp, (row // HALF) % NZ, row // LINE)
        hot = jnp.where(hot, 1.0, 0.0).astype(jnp.bfloat16)
        hot = jnp.concatenate([hot] * (2 * NX), axis=0)
        keys = jnp.concatenate([kv[yp, :, :, :, :, 0:HD].reshape(PIECE, HD), hot], axis=1)
        values = jnp.concatenate(
            [kv[yp, :, :, :, :, HD : 2 * HD].reshape(PIECE, HD), jnp.ones((PIECE, HD), jnp.bfloat16)], axis=1
        )

        def score(place):
            return lax.dot_general(
                qa[aligned(place * TILE, TILE), :], keys, (((1,), (1,)), ((), ())), preferred_element_type=jnp.float32
            )

        places = [pick(half * 2), pick(half * 2 + 1)]
        ahead = score(places[0])
        for j, place in enumerate(places):
            rows = aligned(place * TILE, TILE)
            scores = ahead
            if j + 1 < len(places):
                ahead = score(places[j + 1])
            old = top[rows, :]
            new = jnp.maximum(old, jnp.max(scores, axis=1, keepdims=True))
            top[rows, :] = new
            weights = jnp.exp2((scores - new[:, 0:1]) * EXPONENT).astype(jnp.bfloat16)
            factor = jnp.exp2((old - new) * EXPONENT)
            total = acc[rows, :] * jnp.concatenate([factor, factor], axis=1) + jnp.dot(
                weights, values, preferred_element_type=jnp.float32
            )
            if finish:
                result[rows, :] = (total[:, 0:HD] / total[:, HD : 2 * HD]).astype(jnp.bfloat16)
                send_tile(place)
            else:
                acc[rows, :] = total

    def queries(k):
        ref = qa.at[aligned(source[k] * TILE, TILE), pl.ds(0, HD)]
        pltpu.make_async_copy(ref, ref, q_sem.at[k]).wait()

    def keys_of(k):
        along_z(k, 0)
        along_z(k, 1)

    actions = dict(

        A=step_a, B=step_b, C=step_c, K=keys_of, Q=lambda k: along_z(k, 2), S=complete, R=queries,
        Y=lambda k: along_y(k, 0), y=lambda k: along_y(k, 1), W=lambda k: from_y(k, 0), w=lambda k: from_y(k, 1),
    )

    def run(text):
        for action, which in zip(text[::2], text[1::2]):
            actions[action](int(which))

    for text in BEFORE:
        run(text)

    @pl.loop(0, 6)
    def _(i):
        for at, text in enumerate(STEPS):

            @pl.when(i == at)
            def _():
                run(text)

        attend(jnp.where(i < 4, i % 2, 2), jnp.where(i < 4, i // 2, i % 2), False)

    run(AFTER)

    @pl.loop(0, 2)
    def _(half):
        attend(3, half, True)

    def done(ref, sem):
        pltpu.make_async_copy(ref, ref, sem).wait()

    done(stage.at[:, :, pl.ds(0, NZ * 2 * HD)], y_send.at[0])
    done(stage.at[:, :, pl.ds(0, NZ * HD)], y_send.at[1])
    done(qa.at[pl.ds(0, QUERIES - NY * ROWS), :], z_send.at[0])
    done(result.at[pl.ds(0, QUERIES - NY * ROWS), :], z_send.at[1])
    for i in range(8):
        ref = kv.at[:, :, 0, 0, pl.ds(0, LINE // 2), :] if i in (3, 4) else kv.at[:, :, 0, 0]
        done(ref, ring_send.at[i])
    done(result.at[pl.ds(0, QUERIES - ROWS), :], out_send.at[0])
    done(result, out_sem.at[0])


def on_device(tokens_qkv, block_mask):
    dma = pltpu.SemaphoreType.DMA
    return pl.pallas_call(
        kernel,
        out_shape=jax.ShapeDtypeStruct((ROWS, NY * NZ * HD), jnp.bfloat16),
        in_specs=[pl.BlockSpec(memory_space=pl.ANY), pl.BlockSpec(memory_space=pl.ANY)],
        out_specs=pl.BlockSpec(memory_space=pl.ANY),
        scratch_shapes=[
            pltpu.VMEM((ROWS, NY * NZ * 3 * HD), jnp.bfloat16),
            pltpu.VMEM((64, 64), jnp.int32),
            pltpu.VMEM((NY - 1, ROWS, NZ * 3 * HD), jnp.bfloat16),
            pltpu.VMEM((NY, 2, NX, NC, LINE, 2 * HD), jnp.bfloat16),
            pltpu.VMEM((QUERIES, 2 * HD), jnp.bfloat16),
            pltpu.VMEM((QUERIES, 2 * HD), jnp.float32),
            pltpu.VMEM((QUERIES, HD), jnp.float32),
            pltpu.VMEM((64, HD), jnp.float32),
            pltpu.VMEM((QUERIES, HD), jnp.bfloat16),
            dma((2,)),
            dma((NY - 1, 2)),
            dma((2,)),
            dma((NY,)),
            dma((NY, 2)),
            dma((2,)),
            dma((NY, 2, NX, NC)),
            dma((8,)),
            dma((1,)),
            dma((1,)),
        ],
        compiler_params=pltpu.CompilerParams(
            collective_id=0, has_side_effects=True, vmem_limit_bytes=62 * 1024 * 1024
        ),
        cost_estimate=pl.CostEstimate(flops=8 * 1024 * 8192 * 128, bytes_accessed=1 << 20, transcendentals=1024 * 8192),
    )(tokens_qkv, block_mask)


def solution(mesh):
    return jax.shard_map(
        on_device,
        mesh=mesh,
        in_specs=(P(("blk", "head"), None), P()),
        out_specs=P(("blk", "head"), None),
        check_vma=False,
    )
```

time: 61.7 us -> 56.1 us (0.909)
  the two profiles are of different devices: /device:TPU:25 before, /device:TPU:1 now
where the time goes in v3:
time: 56.1 us; the launch traced here: 55.9 us
  Pallas kernels  54.2 us (97%)
  local copies, waits for them, and re-layouts  1.67 us (3%)
    pallas_call x1, Pallas kernels, on_device(): pl.pallas_call(kernel, out_shape=jax.ShapeDtypeStruct((ROWS, NY * NZ * HD...  54.2 us
    unnamed x1, local copies, waits for them, and re-layouts  1.67 us

profile of v3, /device:TPU:1, one launch (start us, length us, event | category | flops | bytes accessed | tf_op | source)
XLA Modules:
  0.0 55.9 jit_solution(11608699866596949983)
XLA Ops:
  0.0 54.2 %shard_map.28 = bf16[32,4096]{1,0:T(8,128)(2,1)} custom-call(bf16[32,12288]{1,0:T(8,128)(2,1)} %tokens.1, s32[64,64]{1,0:T(8,128)} %mask.1), custom_call_target="tpu_custom_call" | custom-call | flops 8589934592 | bytes 1048576 | tf_op jit(solution)/shard_map/pallas_call | solution.py:280
  54.2 1.7 %copy.4 = bf16[32,4096]{1,0:T(8,128)(2,1)} copy(bf16[32,4096]{1,0:T(8,128)(2,1)} %shard_map.28) | data formatting | bytes 524288

commit v4 on v3

--- a/solution.py
+++ b/solution.py
@@ -186,7 +186,7 @@
                     device_id=device_at(x, j, pz, c), device_id_type=MESH,
                 ).start()
 
-    def attend(k, half, finish):
+    def attend(k, tiles, finish):
         yp = pick(k)
         row = lax.broadcasted_iota(jnp.int32, (NC * LINE, HD), 0)
         col = lax.broadcasted_iota(jnp.int32, (NC * LINE, HD), 1)
@@ -203,7 +203,7 @@
                 qa[aligned(place * TILE, TILE), :], keys, (((1,), (1,)), ((), ())), preferred_element_type=jnp.float32
             )
 
-        places = [pick(half * 2), pick(half * 2 + 1)]
+        places = [pick(t) for t in tiles]
         ahead = score(places[0])
         for j, place in enumerate(places):
             rows = aligned(place * TILE, TILE)
@@ -253,13 +253,12 @@
             def _():
                 run(text)
 
-        attend(jnp.where(i < 4, i % 2, 2), jnp.where(i < 4, i // 2, i % 2), False)
+        half = jnp.where(i < 4, i // 2, i % 2)
+        attend(jnp.where(i < 4, i % 2, 2), (half * 2, half * 2 + 1), False)
 
     run(AFTER)
 
-    @pl.loop(0, 2)
-    def _(half):
-        attend(3, half, True)
+    attend(3, range(NY), True)
 
     def done(ref, sem):
         pltpu.make_async_copy(ref, ref, sem).wait()

time: 56.1 us -> 55.8 us (level)
  no operation moved by 1% of the time
where the time goes in v4:
time: 55.8 us; the launch traced here: 55.7 us
  Pallas kernels  54 us (97%)
  local copies, waits for them, and re-layouts  1.67 us (3%)
    pallas_call x1, Pallas kernels, on_device(): pl.pallas_call(kernel, out_shape=jax.ShapeDtypeStruct((ROWS, NY * NZ * HD...  54 us
    unnamed x1, local copies, waits for them, and re-layouts  1.67 us

profile of v4, /device:TPU:1, one launch (start us, length us, event | category | flops | bytes accessed | tf_op | source)
XLA Modules:
  0.0 55.7 jit_solution(12987899444056995238)
XLA Ops:
  0.0 54.0 %shard_map.28 = bf16[32,4096]{1,0:T(8,128)(2,1)} custom-call(bf16[32,12288]{1,0:T(8,128)(2,1)} %tokens.1, s32[64,64]{1,0:T(8,128)} %mask.1), custom_call_target="tpu_custom_call" | custom-call | flops 8589934592 | bytes 1048576 | tf_op jit(solution)/shard_map/pallas_call | solution.py:279
  54.0 1.7 %copy.4 = bf16[32,4096]{1,0:T(8,128)(2,1)} copy(bf16[32,4096]{1,0:T(8,128)(2,1)} %shard_map.28) | data formatting | bytes 524288

commit v5 on v4

--- a/solution.py
+++ b/solution.py
@@ -213,7 +213,7 @@
             old = top[rows, :]
             new = jnp.maximum(old, jnp.max(scores, axis=1, keepdims=True))
             top[rows, :] = new
-            weights = jnp.exp2((scores - new[:, 0:1]) * EXPONENT).astype(jnp.bfloat16)
+            weights = jnp.exp2(scores * EXPONENT - new[:, 0:1] * EXPONENT).astype(jnp.bfloat16)
             factor = jnp.exp2((old - new) * EXPONENT)
             total = acc[rows, :] * jnp.concatenate([factor, factor], axis=1) + jnp.dot(
                 weights, values, preferred_element_type=jnp.float32

time: 55.8 us -> 56 us (level)
  no operation moved by 1% of the time
where the time goes in v5:
time: 56 us; the launch traced here: 55.8 us
  Pallas kernels  54.2 us (97%)
  local copies, waits for them, and re-layouts  1.67 us (3%)
    pallas_call x1, Pallas kernels, on_device(): pl.pallas_call(kernel, out_shape=jax.ShapeDtypeStruct((ROWS, NY * NZ * HD...  54.2 us
    unnamed x1, local copies, waits for them, and re-layouts  1.67 us

profile of v5, /device:TPU:1, one launch (start us, length us, event | category | flops | bytes accessed | tf_op | source)
XLA Modules:
  0.0 55.8 jit_solution(4573889450873591232)
XLA Ops:
  0.0 54.2 %shard_map.28 = bf16[32,4096]{1,0:T(8,128)(2,1)} custom-call(bf16[32,12288]{1,0:T(8,128)(2,1)} %tokens.1, s32[64,64]{1,0:T(8,128)} %mask.1), custom_call_target="tpu_custom_call" | custom-call | flops 8589934592 | bytes 1048576 | tf_op jit(solution)/shard_map/pallas_call | solution.py:279
  54.2 1.7 %copy.4 = bf16[32,4096]{1,0:T(8,128)(2,1)} copy(bf16[32,4096]{1,0:T(8,128)(2,1)} %shard_map.28) | data formatting | bytes 524288
